TPU v7x, 256 devices: a whole 4x4x8 slice. The times are simulated.
256 devices in a mesh: tile: 32 (over y, z_lo, core), freq: 8 (over z_hi, x).
Axes of the slice: x: 4, y: 4, z: 8 (z_hi: 2, z_lo: 4; z = z_hi * 4 + z_lo), core: 2. Of those that a mesh axis runs over, the one named last changes fastest.
Arguments:
- leaf_maps: bfloat16 [8, 65536, 2048], P('freq', 'tile'), as said below
- wave_index: int32 [8], P('freq'), may hold values from 0 to 7, as said below
- medium: bfloat16 [16384, 512], P('tile'), may hold values from 0.5 to 2
- source: bfloat16 [8, 16384, 512], P('freq', 'tile'), may hold values from -6 to 6
- state_field: bfloat16 [8, 16384, 512], P('freq', 'tile'), may hold values from -6 to 6
- adjoint_field: bfloat16 [8, 16384, 512], P('freq', 'tile'), may hold values from -6 to 6
- receivers: int32 [8, 8192], P('freq', 'tile'), may hold values from 0 to 262143
- recorded: bfloat16 [8, 8192], P('freq', 'tile'), may hold values from -180 to 180
Outputs:
- merged_maps: bfloat16 [8, 16384, 2048], P('freq', 'tile')
- medium_gradient: float32 [16384, 512], P(('tile', 'freq'))
Inputs may be any that keep to these rules, and one draw needn't show every extreme that they name: leaf_maps: every leaf box map is exactly symmetric and positive definite. wave_index: the first eight frequencies (all of them if fewer) have distinct values.
All inputs are finite; a program needn't handle non-finite values.
Results may differ from a plain program's by a relative error of at most 0.0082.
Values may be sent and summed in bfloat16 or wider, within the bound.
No kernel may reach another device: no remote copies, remote signals or barrier semaphores. Data moves between devices by JAX's collectives and lax.ppermute only.
A program may use at most 192 MiB of HBM per device.

v0:
```python
import jax
import jax.numpy as jnp
from jax import lax
from jax.sharding import PartitionSpec as P


def from_partner(block, axis, distance):
    count = lax.axis_size(axis)
    route = []
    for low in range(count):
        high = low | 1 << distance
        if high != low and high < count:
            route += [(low, high), (high, low)]
    return lax.ppermute(block, axis, route)


def extended(block, sides, width):
    for axis, dim in sides:
        count = lax.axis_size(axis)
        forward = [(i, i + 1) for i in range(count - 1)]
        backward = [(target, source) for source, target in forward]
        low = lax.ppermute(
            lax.slice_in_dim(block, block.shape[dim] - width, None, axis=dim), axis, forward
        )
        high = lax.ppermute(lax.slice_in_dim(block, 0, width, axis=dim), axis, backward)
        block = jnp.concatenate([low, block, high], axis=dim)
    return block


def ordered(flag, own_part, partner, axis_number):
    return jnp.where(
        flag == 0,
        jnp.concatenate([own_part, partner], axis=axis_number),
        jnp.concatenate([partner, own_part], axis=axis_number),
    )


def placed(flag, own_block, total_width):
    zero_block = jnp.zeros((own_block.shape[0], total_width - own_block.shape[1]), jnp.float32)
    return ordered(flag, own_block, zero_block, 1)


def triangular(factor, right_side):
    return jax.scipy.linalg.solve_triangular(factor, right_side, lower=True)


def level_one(leaf_map, low_bit):
    half_size = leaf_map.shape[0] // 2
    own_inner = leaf_map[half_size:, half_size:]
    own_coupling = leaf_map[:half_size, half_size:].T.astype(jnp.float32)
    partner_inner = from_partner(own_inner, "tile", 0)
    schur = own_inner.astype(jnp.float32) + partner_inner.astype(jnp.float32)
    factor = jnp.linalg.cholesky(schur)
    solved_own = triangular(factor, own_coupling).astype(jnp.bfloat16)
    solved_partner = from_partner(solved_own, "tile", 0)
    solved_all = ordered(low_bit, solved_own, solved_partner, 1)
    coupling = lax.dot_general(
        solved_own, solved_all, (((0,), (0,)), ((), ())), preferred_element_type=jnp.float32
    )
    own_block = leaf_map[:half_size, :half_size].astype(jnp.float32)
    return (placed(low_bit, own_block, 2 * half_size) - coupling).astype(jnp.bfloat16)


def level_two(own_rows, low_bit, high_bit):
    half_size = own_rows.shape[0]
    quarter = half_size // 2
    inner_cols = jnp.concatenate(
        [own_rows[:, quarter:half_size], own_rows[:, half_size + quarter :]], axis=1
    )
    outer_cols = jnp.concatenate(
        [own_rows[:, :quarter], own_rows[:, half_size : half_size + quarter]], axis=1
    )
    inner_piece = inner_cols[quarter:]
    sibling_piece = from_partner(inner_piece, "tile", 1)
    half_sum = inner_piece.astype(jnp.float32) + sibling_piece.astype(jnp.float32)
    partner_sum = from_partner(half_sum, "tile", 0)
    schur = ordered(low_bit, half_sum, partner_sum, 0)
    factor = jnp.linalg.cholesky(schur)
    solved_own = triangular(factor, inner_cols[:quarter].T.astype(jnp.float32)).astype(jnp.bfloat16)
    solved_partner = from_partner(solved_own, "tile", 0)
    solved_pair = ordered(low_bit, solved_own, solved_partner, 1)
    solved_sibling = from_partner(solved_pair, "tile", 1)
    solved_all = ordered(high_bit, solved_pair, solved_sibling, 1)
    coupling = lax.dot_general(
        solved_own, solved_all, (((0,), (0,)), ((), ())), preferred_element_type=jnp.float32
    )
    own_block = outer_cols[:quarter].astype(jnp.float32)
    return (placed(high_bit, own_block, 2 * half_size) - coupling).astype(jnp.bfloat16)


def stencil(padded, field):
    edges = (
        padded[..., 2:, 1:-1]
        + padded[..., :-2, 1:-1]
        + padded[..., 1:-1, 2:]
        + padded[..., 1:-1, :-2]
    )
    corners = (
        padded[..., 2:, 2:] + padded[..., 2:, :-2] + padded[..., :-2, 2:] + padded[..., :-2, :-2]
    )
    return (4.0 * edges + corners - 20.0 * field) / 6.0


def body(leaf_maps, wave_index, medium, source, state_field, adjoint_field, receivers, recorded):
    tile_index = lax.axis_index("tile")
    low_bit = jnp.bitwise_and(tile_index, 1)
    high_bit = jnp.bitwise_and(jnp.right_shift(tile_index, 1), 1)
    stacked = jnp.stack([state_field, adjoint_field])
    rimmed = extended(stacked, (("tile", 2),), 1)
    rimmed = jnp.pad(rimmed.astype(jnp.float32), ((0, 0), (0, 0), (0, 0), (1, 1)))
    pair_rows = level_one(leaf_maps[0], low_bit)
    merged_list = [level_two(pair_rows, low_bit, high_bit)]
    merged_maps = jnp.stack(merged_list)
    fields = stacked.astype(jnp.float32)
    kappa = 0.2 * (1.0 + wave_index.astype(jnp.float32))
    kappa_sq = (kappa * kappa)[:, None, None]
    medium_full = medium.astype(jnp.float32)[None]
    applied = stencil(rimmed, fields) + kappa_sq[None] * medium_full[None] * fields
    state_full = fields[0]
    adjoint_full = fields[1]
    state_residual = source.astype(jnp.float32) - applied[0]
    box_cells = state_full.shape[1] * state_full.shape[2]
    flat_state = state_full.reshape(state_full.shape[0], box_cells)
    misfit = jnp.take_along_axis(flat_state, receivers, axis=1) - recorded.astype(jnp.float32)
    freq_rows = jnp.broadcast_to(
        jnp.arange(receivers.shape[0], dtype=jnp.int32)[:, None], receivers.shape
    )
    adjoint_source = (
        jnp.zeros(flat_state.shape, jnp.float32)
        .at[freq_rows, receivers]
        .add(misfit)
        .reshape(state_full.shape)
    )
    adjoint_residual = adjoint_source - applied[1]
    gradient_term = -jnp.sum(
        kappa_sq * (state_full * state_residual + adjoint_full * adjoint_residual), axis=0
    )
    share_rows = gradient_term.shape[0] // lax.axis_size("freq")
    total = lax.psum(gradient_term, "freq")
    medium_gradient = lax.dynamic_slice_in_dim(
        total, lax.axis_index("freq") * share_rows, share_rows, 0
    )
    return (merged_maps, medium_gradient)


def solution(mesh):
    placed = (
        P("freq", "tile", None),
        P("freq"),
        P("tile", None),
        P("freq", "tile", None),
        P("freq", "tile", None),
        P("freq", "tile", None),
        P("freq", "tile"),
        P("freq", "tile"),
    )
    return jax.shard_map(
        body,
        mesh=mesh,
        in_specs=placed,
        out_specs=(P("freq", "tile", None), P(("tile", "freq"), None)),
        check_vma=False,
    )
```

profile of v0, /device:TPU:8, one launch (start us, length us, event | category | flops | bytes accessed | tf_op | source)
XLA Modules:
  0.0 1019.8 jit_solution(1663486768981271315)
XLA Ops:
  7.2 12.3 %copy.32 = bf16[1,2048,2048]{1,2,0:T(8,128)(2,1)} copy(bf16[1,2048,2048]{2,1,0:T(8,128)(2,1)} %param.9) | data formatting | bytes 16777216 | tf_op args[0]
  19.5 8.0 fusion.210
  36.3 5.6 copy.33
  47.9 11.7 %cholesky.619 = f32[128,128]{1,0:T(8,128)S(1)} custom-call(f32[128,128]{1,0:T(8,128)S(1)} %cholesky.911), custom_call_target="Cholesky" | custom-call | tf_op jit(solution)/shard_map/jit(cholesky)/cholesky | solution.py:53
  59.6 9.8 custom-call.61
  75.9 12.2 %cholesky.638 = f32[128,128]{1,0:T(8,128)S(1)} custom-call(f32[128,128]{1,0:T(8,128)S(1)} %cholesky.915), custom_call_target="Cholesky" | custom-call | tf_op jit(solution)/shard_map/jit(cholesky)/cholesky | solution.py:53
  88.7 9.8 custom-call.62
  101.9 11.7 %cholesky.659 = f32[128,128]{1,0:T(8,128)S(1)} custom-call(f32[128,128]{1,0:T(8,128)S(1)} %cholesky.920), custom_call_target="Cholesky" | custom-call | tf_op jit(solution)/shard_map/jit(cholesky)/cholesky | solution.py:53
  114.9 9.8 custom-call.63
  128.2 11.9 %cholesky.678 = f32[128,128]{1,0:T(8,128)S(1)} custom-call(f32[128,128]{1,0:T(8,128)S(1)} %cholesky.925), custom_call_target="Cholesky" | custom-call | tf_op jit(solution)/shard_map/jit(cholesky)/cholesky | solution.py:53
  141.5 9.8 custom-call.64
  154.7 11.7 %cholesky.697 = f32[128,128]{1,0:T(8,128)S(1)} custom-call(f32[128,128]{1,0:T(8,128)S(1)} %cholesky.930), custom_call_target="Cholesky" | custom-call | tf_op jit(solution)/shard_map/jit(cholesky)/cholesky | solution.py:53
  167.7 10.0 custom-call.65
  181.1 11.7 %cholesky.716 = f32[128,128]{1,0:T(8,128)S(1)} custom-call(f32[128,128]{1,0:T(8,128)S(1)} %cholesky.935), custom_call_target="Cholesky" | custom-call | tf_op jit(solution)/shard_map/jit(cholesky)/cholesky | solution.py:53
  194.1 9.8 custom-call.66
  206.9 12.1 %cholesky.735 = f32[128,128]{1,0:T(8,128)S(1)} custom-call(f32[128,128]{1,0:T(8,128)S(1)} %cholesky.940), custom_call_target="Cholesky" | custom-call | tf_op jit(solution)/shard_map/jit(cholesky)/cholesky | solution.py:53
  220.3 9.8 custom-call.67
  232.7 11.7 %cholesky.752 = f32[128,128]{1,0:T(8,128)S(1)} custom-call(f32[128,128]{1,0:T(8,128)S(1)} %slice_subtract_fusion.13), custom_call_target="Cholesky" | custom-call | tf_op jit(solution)/shard_map/jit(cholesky)/cholesky | solution.py:53
  251.4 4.8 select_select_fusion.1
  256.3 22.8 %while.2 = (s32[]{:T(128)}, f32[1024,1024]{1,0:T(8,128)}, s32[8,2]{0,1:T(2,128)S(1)}, f32[8,128,128]{2,1,0:T(8,128)S(1)}, s32[]{:T(128)}) while((s32[]{:T(128)}, f32[1024,1024]{1,0:T(8,128)}, s32[8,2]{0,1:T(2,128)S(1)}, f32[8,128,128]{2,1,0:T(8,128)S(1)}, s32[]{:T(128)}) %tuple.122), condition=%wide.while_cond, body=%wide.while_body.sunk | while | flops 2 | bytes 131181 | solution.py:44
  279.1 78.8 %custom-call.52 = f32[8,128,128]{1,2,0:T(8,128)S(1)} custom-call(f32[8,128,128]{2,1,0:T(8,128)S(1)} %get-tuple-element.10), custom_call_target="InvertDiagBlocksLowerTriangular" | custom-call | tf_op jit(solution)/shard_map/jit(_solve_triangular)/triangular_solve | solution.py:44
  387.4 4.9 convolution_subtract_fusion.3
  404.0 10.0 subtract_convert_fusion
  419.8 23.5 %collective-permute-done.2 = bf16[512,1024]{0,1:T(8,128)(2,1)S(1)} collective-permute-done((bf16[512,1024]{0,1:T(8,128)(2,1)S(1)}, bf16[512,1024]{0,1:T(8,128)(2,1)S(1)}, u32[]{:S(2)}, u32[]{:S(2)}) %collective-permute-start.2) | collective-permute-done | bytes 1048608 | tf_op jit(solution)/shard_map/ppermute | solution.py:14
  447.9 5.8 collective-permute-start.7
  456.9 6.5 maximum_select_fusion.2
  463.5 5.5 copy.43
  475.4 11.7 %cholesky.767 = f32[128,128]{1,0:T(8,128)S(1)} custom-call(f32[128,128]{1,0:T(8,128)S(1)} %cholesky.944), custom_call_target="Cholesky" | custom-call | tf_op jit(solution)/shard_map/jit(cholesky)/cholesky | solution.py:78
  489.6 9.8 custom-call.68
  504.2 11.9 %cholesky.786 = f32[128,128]{1,0:T(8,128)S(1)} custom-call(f32[128,128]{1,0:T(8,128)S(1)} %cholesky.948), custom_call_target="Cholesky" | custom-call | tf_op jit(solution)/shard_map/jit(cholesky)/cholesky | solution.py:78
  518.1 9.8 custom-call.69
  532.9 13.2 %cholesky.807 = f32[128,128]{1,0:T(8,128)} custom-call(f32[128,128]{1,0:T(8,128)} %cholesky.953), custom_call_target="Cholesky" | custom-call | tf_op jit(solution)/shard_map/jit(cholesky)/cholesky | solution.py:78
  548.2 11.3 %custom-call.70 = f32[1,128,128]{1,2,0:T(8,128)} custom-call(f32[1,128,128]{2,1,0:T(8,128)} %get-tuple-element.105), custom_call_target="InvertDiagBlocksLowerTriangular" | custom-call | tf_op jit(solution)/shard_map/jit(cholesky)/cholesky | solution.py:78
  563.8 12.7 %cholesky.826 = f32[128,128]{1,0:T(8,128)} custom-call(f32[128,128]{1,0:T(8,128)S(1)} %cholesky.958), custom_call_target="Cholesky" | custom-call | tf_op jit(solution)/shard_map/jit(cholesky)/cholesky | solution.py:78
  578.6 10.4 %custom-call.71 = f32[1,128,128]{1,2,0:T(8,128)} custom-call(f32[1,128,128]{2,1,0:T(8,128)S(1)} %get-tuple-element.102), custom_call_target="InvertDiagBlocksLowerTriangular" | custom-call | tf_op jit(solution)/shard_map/jit(cholesky)/cholesky | solution.py:78
  593.4 11.7 %cholesky.845 = f32[128,128]{1,0:T(8,128)S(1)} custom-call(f32[128,128]{1,0:T(8,128)S(1)} %cholesky.963), custom_call_target="Cholesky" | custom-call | tf_op jit(solution)/shard_map/jit(cholesky)/cholesky | solution.py:78
  606.4 10.0 custom-call.72
  619.6 11.7 %cholesky.864 = f32[128,128]{1,0:T(8,128)S(1)} custom-call(f32[128,128]{1,0:T(8,128)S(1)} %cholesky.968), custom_call_target="Cholesky" | custom-call | tf_op jit(solution)/shard_map/jit(cholesky)/cholesky | solution.py:78
  632.6 9.8 custom-call.73
  645.4 11.9 %cholesky.883 = f32[128,128]{1,0:T(8,128)S(1)} custom-call(f32[128,128]{1,0:T(8,128)S(1)} %cholesky.973), custom_call_target="Cholesky" | custom-call | tf_op jit(solution)/shard_map/jit(cholesky)/cholesky | solution.py:78
  658.6 9.8 custom-call.74
  671.1 11.7 %cholesky.900 = f32[128,128]{1,0:T(8,128)S(1)} custom-call(f32[128,128]{1,0:T(8,128)S(1)} %slice_subtract_fusion.12), custom_call_target="Cholesky" | custom-call | tf_op jit(solution)/shard_map/jit(cholesky)/cholesky | solution.py:78
  689.0 4.8 select_select_fusion
  694.6 28.1 %while.3 = (s32[]{:T(128)}, f32[1024,1024]{1,0:T(8,128)}, s32[8,2]{0,1:T(2,128)S(1)}, f32[8,128,128]{2,1,0:T(8,128)}, s32[]{:T(128)}) while((s32[]{:T(128)}, f32[1024,1024]{1,0:T(8,128)}, s32[8,2]{0,1:T(2,128)S(1)}, f32[8,128,128]{2,1,0:T(8,128)}, s32[]{:T(128)}) %tuple.130), condition=%wide.while_cond.1, body=%wide.while_body.1.sunk | while | flops 2 | bytes 132705 | solution.py:44
  722.7 80.4 %custom-call.53 = f32[8,128,128]{1,2,0:T(8,128)} custom-call(f32[8,128,128]{2,1,0:T(8,128)} %get-tuple-element.18), custom_call_target="InvertDiagBlocksLowerTriangular" | custom-call | tf_op jit(solution)/shard_map/jit(_solve_triangular)/triangular_solve | solution.py:44
  869.9 4.6 maximum_select_fusion.11
  879.8 121.3 %all-reduce.9.cloned.1.call-done = f32[512,512]{1,0:T(8,128)} async-done(((f32[512,512]{1,0:T(8,128)}), f32[512,512]{1,0:T(8,128)}) %all-reduce.9.cloned.1.call-update) | async-done | bytes 1048592 | tf_op jit(solution)/shard_map/psum | solution.py:139
  1004.0 6.4 fusion.16
  (254 shorter events, 279.8 us)
Async XLA Ops:
  7.2 993.9 %all-reduce.9.cloned.1.call-start = ((), (), s32[]{:S(2)}) async-start(), calls=%async_computation | async-start | bytes 2097152 | tf_op jit(solution)/shard_map/psum | solution.py:139
  27.5 4.4 collective-permute-start
  45.9 1.9 copy-start.1
  399.6 4.4 collective-permute-start.1
  417.8 27.0 %copy-start.2 = (bf16[1,512,512]{2,1,0:T(8,128)(2,1)S(1)}, bf16[1,512,512]{2,1,0:T(8,128)(2,1)}, u32[]{:S(2)}) copy-start(bf16[1,512,512]{2,1,0:T(8,128)(2,1)} %param.14) | copy-start | bytes 1572868
  417.8 27.0 %copy-start.3 = (bf16[1,512,512]{2,1,0:T(8,128)(2,1)S(1)}, bf16[1,512,512]{2,1,0:T(8,128)(2,1)}, u32[]{:S(2)}) copy-start(bf16[1,512,512]{2,1,0:T(8,128)(2,1)} %param.13) | copy-start | bytes 1572868
  417.8 25.4 %collective-permute-start.2 = (bf16[512,1024]{0,1:T(8,128)(2,1)S(1)}, bf16[512,1024]{0,1:T(8,128)(2,1)S(1)}, u32[]{:S(2)}, u32[]{:S(2)}) collective-permute-start(bf16[512,1024]{0,1:T(8,128)(2,1)S(1)} %get-tuple-element.53), channel_id=1, source_target_pairs={{0,16},{16,0},{8,24},{24,8},{32,48},{48,32},{40,56},{56,40},{64,80... | collective-permute-start | bytes 3145736 | tf_op jit(solution)/shard_map/ppermute | solution.py:14
  444.8 12.1 %collective-permute-start.3 = (f32[512,1024]{0,1:T(8,128)}, f32[512,1024]{0,1:T(8,128)}, u32[]{:S(2)}, u32[]{:S(2)}) collective-permute-start(f32[512,1024]{0,1:T(8,128)} %convert_add_fusion.1), channel_id=1, source_target_pairs={{0,8},{8,0},{16,24},{24,16},{32,40},{40,32},{48,56},{56,48},{64,72... | collective-permute-start | bytes 6291464 | tf_op jit(solution)/shard_map/ppermute | solution.py:14
  445.5 423.3 %collective-permute-start.6 = (bf16[2,1,1,512]{3,2,1,0:T(2,128)(2,1)}, bf16[2,1,1,512]{3,2,1,0:T(2,128)(2,1)S(1)}, u32[]{:S(2)}, u32[]{:S(2)}) collective-permute-start(bf16[2,1,1,512]{3,2,1,0:T(2,128)(2,1)} %get-tuple-element.54), channel_id=1, source_target_pairs={{0,8},{8,16},{16,24},{24,32},{32,40},{40,48},{48,56},{56,64},{64,7... | collective-permute-start | bytes 6152 | tf_op jit(solution)/shard_map/ppermute | solution.py:22
  447.9 420.9 %collective-permute-start.7 = (bf16[2,1,1,512]{3,2,1,0:T(2,128)(2,1)S(1)}, bf16[2,1,1,512]{3,2,1,0:T(2,128)(2,1)}, u32[]{:S(2)}, u32[]{:S(2)}) collective-permute-start(bf16[2,1,1,512]{3,2,1,0:T(2,128)(2,1)S(1)} %get-tuple-element.55), channel_id=1, source_target_pairs={{8,0},{16,8},{24,16},{32,24},{40,32},{48,40},{56,48},{64,56},{72,6... | collective-permute-start | bytes 6152 | tf_op jit(solution)/shard_map/ppermute | solution.py:25
  454.4 1.5 copy-start.12
  473.4 1.9 copy-start
  503.3 0.8 copy-start.9
  808.9 7.8 copy-start.6
  812.6 4.0 copy-start.8
  816.7 0.7 copy-start.10
  834.5 25.9 %copy-start.13 = (s32[1,256,1]{1,2,0:T(1,128)S(1)}, s32[1,256,1]{1,2,0:T(1,128)}, u32[]{:S(2)}) copy-start(s32[1,256,1]{1,2,0:T(1,128)} %fusion.242) | copy-start | bytes 3076
  856.6 13.3 %collective-permute-start.4 = (bf16[1024,512]{0,1:T(8,128)(2,1)}, bf16[1024,512]{0,1:T(8,128)(2,1)}, u32[]{:S(2)}, u32[]{:S(2)}) collective-permute-start(bf16[1024,512]{0,1:T(8,128)(2,1)} %fusion.48), channel_id=1, source_target_pairs={{0,8},{8,0},{16,24},{24,16},{32,40},{40,32},{48,56},{56,48},{64,72... | collective-permute-start | bytes 3145736 | tf_op jit(solution)/shard_map/ppermute | solution.py:14
  868.8 5.7 copy-start.4
  874.4 3.6 copy-start.5
  874.4 3.6 copy-start.11
  874.4 129.5 %collective-permute-start.5 = (bf16[1024,1024]{0,1:T(8,128)(2,1)}, bf16[1024,1024]{0,1:T(8,128)(2,1)}, u32[]{:S(2)}, u32[]{:S(2)}) collective-permute-start(bf16[1024,1024]{0,1:T(8,128)(2,1)} %maximum_select_fusion.11), channel_id=1, source_target_pairs={{0,16},{16,0},{8,24},{24,8},{32,48},{48,32},{40,56},{56,40},{64,80... | collective-permute-start | bytes 6291464 | tf_op jit(solution)/shard_map/ppermute | solution.py:14
  878.1 124.6 %copy-start.7 = (bf16[1024,512]{0,1:T(8,128)(2,1)S(1)}, bf16[1024,512]{0,1:T(8,128)(2,1)}, u32[]{:S(2)}) copy-start(bf16[1024,512]{0,1:T(8,128)(2,1)} %get-tuple-element.49) | copy-start | bytes 3145732
Sparse Core Ops, SparseCore 0:
  879.9 121.1 all-reduce.8
where the time goes:
time: 1030 us; the launch traced here: 1020 us
  other arithmetic  572 us (56%)
  waiting for transfers between devices  153 us (15%)
  matrix products  133 us (13%)
  local copies, waits for them, and re-layouts  125 us (12%)
  between operations  25.5 us (2%)
  starting transfers between devices  10.4 us (1%)
    another operation x31, other arithmetic, level_two(): factor = jnp.linalg.cholesky(schur)  179 us
    another operation x30, other arithmetic, level_one(): factor = jnp.linalg.cholesky(schur)  173 us
    another operation x5, other arithmetic, triangular(): return jax.scipy.linalg.solve_triangular(factor, right_side, lower=True)  169 us
    psum x1, waiting for transfers between devices, body(): total = lax.psum(gradient_term, 'freq')  121 us
    another operation x30, matrix products, triangular(): return jax.scipy.linalg.solve_triangular(factor, right_side, lower=True)  67.7 us
    another operation x48, local copies, waits for them, and re-layouts  50.8 us
    unnamed x48, local copies, waits for them, and re-layouts  37.5 us
    ppermute x6, waiting for transfers between devices, from_partner(): return lax.ppermute(block, axis, route)  32.1 us
  transfers between devices with their start and end apart: 9, of which 4 were waited for; matrix products, arithmetic and copies ran while one was open for 41% of the time, Pallas kernels for 0%

commit v1 on v0

v1 whole, which is shorter than its diff:
```python
import functools

import jax
import jax.numpy as jnp
from jax import lax
from jax.experimental import pallas as pl
from jax.experimental.pallas import tpu as pltpu
from jax.sharding import PartitionSpec as P

BLOCK = 128
SUB = 8
CHUNK = 256
VMEM_LIMIT = 56 * 1024 * 1024


def from_partner(block, axis, distance):
    count = lax.axis_size(axis)
    route = []
    for low in range(count):
        high = low | 1 << distance
        if high != low and high < count:
            route += [(low, high), (high, low)]
    return lax.ppermute(block, axis, route)


def extended(block, sides, width):
    for axis, dim in sides:
        count = lax.axis_size(axis)
        forward = [(i, i + 1) for i in range(count - 1)]
        backward = [(target, source) for source, target in forward]
        low = lax.ppermute(
            lax.slice_in_dim(block, block.shape[dim] - width, None, axis=dim), axis, forward
        )
        high = lax.ppermute(lax.slice_in_dim(block, 0, width, axis=dim), axis, backward)
        block = jnp.concatenate([low, block, high], axis=dim)
    return block


def ordered(flag, own_part, partner, axis_number):
    return jnp.where(
        flag == 0,
        jnp.concatenate([own_part, partner], axis=axis_number),
        jnp.concatenate([partner, own_part], axis=axis_number),
    )


def placed(flag, own_block, total_width):
    zero_block = jnp.zeros((own_block.shape[0], total_width - own_block.shape[1]), jnp.float32)
    return ordered(flag, own_block, zero_block, 1)


def split(x):
    high = x.astype(jnp.bfloat16)
    return high, (x - high.astype(jnp.float32)).astype(jnp.bfloat16)


def dot(a, b):
    return lax.dot_general(a, b, (((1,), (0,)), ((), ())), preferred_element_type=jnp.float32)


def lane_broadcast(x, lane):
    return jnp.broadcast_to(x[:, lane : lane + 1], x.shape)


def inverse_factor(rows):
    rows = list(rows)
    shape = rows[0].shape
    lane = lax.broadcasted_iota(jnp.int32, shape, 1)
    sub = lax.broadcasted_iota(jnp.int32, shape, 0)
    count = len(rows)
    for s in range(count):
        base = SUB * s
        pivots = (lane >= base) & (lane < base + SUB)
        spread = [jnp.broadcast_to(rows[s][a : a + 1, :], shape) for a in range(SUB)]
        entry = {
            (a, b): lane_broadcast(spread[a], base + b) for a in range(SUB) for b in range(a, SUB)
        }
        right = [
            jnp.where(pivots, jnp.where(lane == base + a, 1.0, 0.0), spread[a]) for a in range(SUB)
        ]
        left = {
            t: [lane_broadcast(rows[t], base + c) for c in range(SUB)] for t in range(s + 1, count)
        }
        scale, done, factor = [], [], {}
        if s + 1 < count:
            column = list(left[s + 1])
            following = jnp.where(pivots, 0.0, rows[s + 1])
        for j in range(SUB):
            r = lax.rsqrt(entry[j, j])
            scale.append(r)
            for b in range(j + 1, SUB):
                factor[b, j] = entry[j, b] * r
            for a in range(j + 1, SUB):
                for b in range(a, SUB):
                    entry[a, b] = entry[a, b] - factor[a, j] * factor[b, j]
            row = right[j] * r
            done.append(row)
            for a in range(j + 1, SUB):
                right[a] = right[a] - factor[a, j] * row
            if s + 1 < count:
                weight = column[j] * r
                for a in range(j + 1, SUB):
                    column[a] = column[a] - weight * factor[a, j]
                following = following - weight * row
        group = done[SUB - 1]
        for a in range(SUB - 1):
            group = jnp.where(sub == a, done[a], group)
        rows[s] = group
        if s + 1 < count:
            rows[s + 1] = following
        if s + 2 < count:
            solved = list(done)
            for c in range(SUB - 1, -1, -1):
                solved[c] = solved[c] * scale[c]
                for a in range(c):
                    solved[a] = solved[a] - factor[c, a] * solved[c]
            for t in range(s + 2, count):
                value = jnp.where(pivots, 0.0, rows[t])
                for c in range(SUB):
                    value = value - left[t][c] * solved[c]
                rows[t] = value
    return [jnp.where(lane <= sub + SUB * s, rows[s], 0.0) for s in range(count)]


def column_chunks(start, stop):
    chunks = []
    while start < stop:
        end = min(stop, (start // CHUNK + 1) * CHUNK)
        chunks.append((start, end))
        start = end
    return chunks


def solve_kernel(own_ref, other_ref, right_ref, out_ref, work_ref, panel_ref, left_ref):
    size, width = right_ref.shape
    blocks = size // BLOCK
    total = size + width
    for i in range(blocks):
        r = slice(i * BLOCK, (i + 1) * BLOCK)
        work_ref[r, i * BLOCK : size] = own_ref[r, i * BLOCK :].astype(jnp.float32) + other_ref[
            r, i * BLOCK :
        ].astype(jnp.float32)
        work_ref[r, size:] = right_ref[r, :].astype(jnp.float32)
    for k in range(blocks):
        start = k * BLOCK
        stop = start + BLOCK
        r = slice(start, stop)
        rows = [
            work_ref[start + SUB * s : start + SUB * (s + 1), start:stop]
            for s in range(BLOCK // SUB)
        ]
        high, low = split(jnp.concatenate(inverse_factor(rows), axis=0))
        both = jnp.concatenate([high, low], axis=1)
        for c0, c1 in column_chunks(stop, total):
            work_high, work_low = split(work_ref[r, c0:c1])
            panel = dot(both, jnp.concatenate([work_high, work_high], axis=0)) + dot(high, work_low)
            panel_high, panel_low = split(panel)
            panel_ref[:BLOCK, c0:c1] = panel_high
            panel_ref[BLOCK:, c0:c1] = panel_low
            if c0 >= size:
                out_ref[c0 - size : c1 - size, r] = panel_high.T
            else:
                for c in range(c0, c1, BLOCK):
                    turned_high, turned_low = split(panel[:, c - c0 : c - c0 + BLOCK].T)
                    left_ref[c : c + BLOCK, :BLOCK] = turned_high
                    left_ref[c : c + BLOCK, BLOCK:] = turned_low
        for i0, i1 in ((k + 1, k + 2), (k + 2, blocks)):
            if i0 >= blocks:
                continue
            for c0, c1 in column_chunks(i0 * BLOCK, total):
                q = slice(i0 * BLOCK, min(i1 * BLOCK, c1))
                panel_high = panel_ref[:BLOCK, c0:c1]
                update = dot(
                    left_ref[q, :], jnp.concatenate([panel_high, panel_high], axis=0)
                ) + dot(left_ref[q, :BLOCK], panel_ref[BLOCK:, c0:c1])
                work_ref[q, c0:c1] = work_ref[q, c0:c1] - update


def solved_columns(own, other, right, own_spec, right_spec, width):
    size = other.shape[0]
    return pl.pallas_call(
        solve_kernel,
        grid=(1,),
        out_shape=jax.ShapeDtypeStruct((width, size), jnp.bfloat16),
        in_specs=[own_spec, pl.BlockSpec((size, size), lambda g: (0, 0)), right_spec],
        out_specs=pl.BlockSpec((width, size), lambda g: (0, 0)),
        scratch_shapes=[
            pltpu.VMEM((size, size + width), jnp.float32),
            pltpu.VMEM((2 * BLOCK, size + width), jnp.bfloat16),
            pltpu.VMEM((size, 2 * BLOCK), jnp.bfloat16),
        ],
        compiler_params=pltpu.CompilerParams(vmem_limit_bytes=VMEM_LIMIT),
        cost_estimate=pl.CostEstimate(
            flops=60_000_000_000, bytes_accessed=8_000_000, transcendentals=0
        ),
    )(own, other, right)


def product(a, b):
    return lax.dot_general(a, b, (((1,), (1,)), ((), ())), preferred_element_type=jnp.float32)


def maps_merged(leaf_map, low_bit, high_bit, partner_inner):
    half = leaf_map.shape[0] // 2
    quarter = half // 2
    solved_own = solved_columns(
        leaf_map,
        partner_inner,
        leaf_map,
        pl.BlockSpec((half, half), lambda g: (1, 1)),
        pl.BlockSpec((half, half), lambda g: (1, 0)),
        half,
    )
    solved_partner = from_partner(solved_own, "tile", 0)
    own_outer, own_inner = solved_own[:quarter], solved_own[quarter:]
    partner_outer, partner_inner = solved_partner[:quarter], solved_partner[quarter:]
    inner_all = ordered(low_bit, own_inner, partner_inner, 0)
    outer_all = ordered(low_bit, own_outer, partner_outer, 0)
    block = leaf_map[:half, :half].astype(jnp.float32)
    inner_rows = (
        placed(low_bit, block[quarter:, quarter:], half) - product(own_inner, inner_all)
    ).astype(jnp.bfloat16)
    sibling_rows = from_partner(inner_rows, "tile", 1)
    sum_rows = inner_rows.astype(jnp.float32) + sibling_rows.astype(jnp.float32)
    outer_rows = (
        placed(low_bit, block[:quarter, :quarter], half) - product(own_outer, outer_all)
    ).astype(jnp.bfloat16)
    zero = jnp.zeros((quarter, quarter), jnp.float32)
    right = (
        ordered(low_bit, block[quarter:, :quarter], zero, 0) - product(inner_all, own_outer)
    ).astype(jnp.bfloat16)
    partner_sum = from_partner(sum_rows, "tile", 0)
    schur = ordered(low_bit, sum_rows, partner_sum, 0)
    solved_own = solved_columns(
        schur,
        jnp.zeros((half, half), jnp.bfloat16),
        right,
        pl.BlockSpec((half, half), lambda g: (0, 0)),
        pl.BlockSpec((half, quarter), lambda g: (0, 0)),
        quarter,
    )
    solved_partner = from_partner(solved_own, "tile", 0)
    solved_pair = ordered(low_bit, solved_own, solved_partner, 0)
    solved_sibling = from_partner(solved_pair, "tile", 1)
    solved_all = ordered(high_bit, solved_pair, solved_sibling, 0)
    own_block = outer_rows.astype(jnp.float32)
    return (placed(high_bit, own_block, 2 * half) - product(solved_own, solved_all)).astype(
        jnp.bfloat16
    )


def stencil(padded, field):
    edges = (
        padded[..., 2:, 1:-1]
        + padded[..., :-2, 1:-1]
        + padded[..., 1:-1, 2:]
        + padded[..., 1:-1, :-2]
    )
    corners = (
        padded[..., 2:, 2:] + padded[..., 2:, :-2] + padded[..., :-2, 2:] + padded[..., :-2, :-2]
    )
    return (4.0 * edges + corners - 20.0 * field) / 6.0


def gradient(wave_index, medium, source, state_field, adjoint_field, receivers, recorded):
    stacked = jnp.stack([state_field, adjoint_field])
    rimmed = extended(stacked, (("tile", 2),), 1)
    rimmed = jnp.pad(rimmed.astype(jnp.float32), ((0, 0), (0, 0), (0, 0), (1, 1)))
    fields = stacked.astype(jnp.float32)
    kappa = 0.2 * (1.0 + wave_index.astype(jnp.float32))
    kappa_sq = (kappa * kappa)[:, None, None]
    medium_full = medium.astype(jnp.float32)[None]
    applied = stencil(rimmed, fields) + kappa_sq[None] * medium_full[None] * fields
    state_full = fields[0]
    adjoint_full = fields[1]
    state_residual = source.astype(jnp.float32) - applied[0]
    box_cells = state_full.shape[1] * state_full.shape[2]
    flat_state = state_full.reshape(state_full.shape[0], box_cells)
    misfit = jnp.take_along_axis(flat_state, receivers, axis=1) - recorded.astype(jnp.float32)
    freq_rows = jnp.broadcast_to(
        jnp.arange(receivers.shape[0], dtype=jnp.int32)[:, None], receivers.shape
    )
    adjoint_source = (
        jnp.zeros(flat_state.shape, jnp.float32)
        .at[freq_rows, receivers]
        .add(misfit)
        .reshape(state_full.shape)
    )
    adjoint_residual = adjoint_source - applied[1]
    gradient_term = -jnp.sum(
        kappa_sq * (state_full * state_residual + adjoint_full * adjoint_residual), axis=0
    )
    return gradient_term


def body(leaf_maps, wave_index, medium, source, state_field, adjoint_field, receivers, recorded):
    tile_index = lax.axis_index("tile")
    low_bit = jnp.bitwise_and(tile_index, 1)
    high_bit = jnp.bitwise_and(jnp.right_shift(tile_index, 1), 1)
    leaf_map = leaf_maps[0]
    half = leaf_map.shape[0] // 2
    partner_inner = from_partner(leaf_map[half:, half:], "tile", 0)
    gradient_term = gradient(
        wave_index, medium, source, state_field, adjoint_field, receivers, recorded
    )
    partner_inner, gradient_term = lax.optimization_barrier((partner_inner, gradient_term))
    medium_gradient = lax.psum_scatter(gradient_term, "freq", scatter_dimension=0, tiled=True)
    merged_maps = maps_merged(leaf_map, low_bit, high_bit, partner_inner)[None]
    return (merged_maps, medium_gradient)


def solution(mesh):
    placed = (
        P("freq", "tile", None),
        P("freq"),
        P("tile", None),
        P("freq", "tile", None),
        P("freq", "tile", None),
        P("freq", "tile", None),
        P("freq", "tile"),
        P("freq", "tile"),
    )
    return jax.shard_map(
        body,
        mesh=mesh,
        in_specs=placed,
        out_specs=(P("freq", "tile", None), P(("tile", "freq"), None)),
        check_vma=False,
    )
```

time: 1030 us -> 267 us (0.26)
  other arithmetic: 572 us -> 22.9 us
  matrix products: 133 us -> 17.4 us
  local copies, waits for them, and re-layouts: 125 us -> 14.8 us
  Pallas kernels: 0 us -> 71.8 us
  waiting for transfers between devices: 153 us -> 111 us
    another operation x67 -> x1, other arithmetic: 521 us -> 0.76 us  [gradient(): stacked = jnp.stack([state_field, adjoint_field])]
    psum x1 -> x0, waiting for transfers between devices: 121 us -> none  [body(): total = lax.psum(gradient_term, 'freq')]
    another operation x58 -> x0, matrix products: 116 us -> none  [the longest x30 67.7 us: triangular(): return jax.scipy.linalg.solve_triangular(factor, right_side, lower=True)]
    pallas_call x0 -> x2, Pallas kernels: none -> 71.8 us  [solved_columns(): pl.pallas_call(solve_kernel, grid=(1,), out_shape=jax.ShapeDtypeStruct((w...]
    another operation x79 -> x0, local copies, waits for them, and re-layouts: 67.9 us -> none
    ppermute x6, waiting for transfers between devices: 32.1 us -> 81.9 us  [from_partner(): return lax.ppermute(block, axis, route)]
    unnamed x48 -> x20, local copies, waits for them, and re-layouts: 37.5 us -> 2.89 us
    reduce_scatter x0 -> x1, waiting for transfers between devices: none -> 28.7 us  [body(): lax.psum_scatter(gradient_term, 'freq', scatter_dimension=0, tiled=True)]
  transfers between devices with their start and end apart: 9 -> 9, of which waited for: 4 -> 5; matrix products, arithmetic and copies ran while one was open for 41% -> 16% of each run, Pallas kernels for 0% -> 0%
where the time goes in v1:
time: 267 us; the launch traced here: 262 us
  waiting for transfers between devices  111 us (42%)
  Pallas kernels  71.8 us (27%)
  other arithmetic  22.9 us (9%)
  matrix products  17.4 us (7%)
  between operations  15.3 us (6%)
  local copies, waits for them, and re-layouts  14.8 us (6%)
  starting transfers between devices  9.43 us (4%)
    ppermute x6, waiting for transfers between devices, from_partner(): return lax.ppermute(block, axis, route)  81.9 us
    pallas_call x2, Pallas kernels, solved_columns(): pl.pallas_call(solve_kernel, grid=(1,), out_shape=jax.ShapeDtypeStruct((w...  71.8 us
    reduce_scatter x1, waiting for transfers between devices, body(): lax.psum_scatter(gradient_term, 'freq', scatter_dimension=0, tiled=True)  28.7 us
    dot_general x4, matrix products, product(): lax.dot_general(a, b, (((1,), (1,)), ((), ())), preferred_element_type=jn...  17.4 us
    ppermute x1, starting transfers between devices, extended(): lax.ppermute(lax.slice_in_dim(block, 0, width, axis=dim), axis, backward)  6.34 us
    slice x1, other arithmetic, body(): partner_inner = from_partner(leaf_map[half:, half:], 'tile', 0)  5.67 us
  transfers between devices with their start and end apart: 9, of which 5 were waited for; matrix products, arithmetic and copies ran while one was open for 16% of the time, Pallas kernels for 0%

profile of v1, /device:TPU:8, one launch (start us, length us, event | category | flops | bytes accessed | tf_op | source)
XLA Modules:
  0.0 262.2 jit_solution(8968735766610299100)
XLA Ops:
  7.2 0.0 reduce-scatter.2.cloned.1.call-start
  7.2 0.8 fusion.37
  8.0 1.9 collective-permute-start.1
  9.9 6.3 %collective-permute-start.2 = (bf16[2,1,1,512]{3,2,1,0:T(2,128)(2,1)S(1)}, bf16[2,1,1,512]{3,2,1,0:T(2,128)(2,1)S(1)}, u32[]{:S(2)}, u32[]{:S(2)}) collective-permute-start(bf16[2,1,1,512]{3,2,1,0:T(2,128)(2,1)S(1)} %get-tuple-element.16), channel_id=1, source_target_pairs={{8,0},{16,8},{24,16},{32,24},{40,32},{48,40},{56,48},{64,56},{72,6... | collective-permute-start | bytes 6152 | tf_op jit(solution)/shard_map/ppermute | solution.py:34
  16.2 0.0 copy-start
  16.3 0.0 copy-start.1
  16.3 5.7 %fusion.45 = (bf16[1024,1024]{1,0:T(8,128)(2,1)}, f32[1024,1024]{1,0:T(8,128)}) fusion(bf16[2048,2048]{1,0:T(8,128)(2,1)} %bitcast.59), kind=kLoop, calls=%fused_computation.81 | loop fusion | flops 1048576 | bytes 10485760 | tf_op jit(solution)/shard_map/slice | solution.py:302
  22.0 0.0 collective-permute-start
  22.0 0.1 fusion.26
  22.1 0.1 slice_bitcast_fusion.3
  22.2 0.4 copy-done.7
  23.3 1.2 copy.10
  24.5 3.2 %gather_fusion = f32[256]{0:T(256)S(1)} fusion(f32[262144]{0:T(1024)} %bitcast.58, s32[1024]{0:T(1024)S(1)} %pad_clamp_fusion), kind=kCustom, calls=%fused_computation | custom fusion | bytes 3072 | tf_op jit(solution)/shard_map/jit(take_along_axis)/gather | solution.py:279
  27.8 2.2 convert_multiply_fusion
  30.0 3.0 %scatter_custom_fusion = f32[262144]{0:T(1024)} fusion(s32[256]{0:T(256)S(1)} %bitcast.64, f32[256]{0:T(256)S(1)} %bitcast.65, f32[]{:T(128)} %constant.18.clone.1), kind=kCustom, calls=%fused_computation.66 | custom fusion | flops 256 | bytes 1048580 | tf_op jit(solution)/shard_map/scatter-add | solution.py:286
  33.0 2.4 reshape.170
  35.5 0.0 collective-permute-done.1
  35.5 0.3 maximum_convert_fusion
  35.8 0.9 copy-done.2
  36.7 3.7 %fusion.14 = f32[2,1,512,512]{3,2,1,0:T(8,128)S(1)} fusion(f32[2,1,514,512]{3,2,1,0:T(8,128)S(1)} %maximum_convert_fusion, f32[512,512]{1,0:T(8,128)S(1)} %copy-done.2, bf16[1,1,512,512]{3,2,1,0:T(8,128)(2,1)S(1)} %bitcast.53, bf16[1,1,512,512]{3,2,1,0:T(8,128)(2,1)S(1)} %bitcast.57), kind=kLoop, calls=%fused_computation.25 | loop fusion | flops 7864320 | bytes 10518528 | tf_op jit(solution)/shard_map/add | solution.py:273
  40.4 1.7 fusion.32
  42.1 0.0 collective-permute-done.other_ref
  42.1 36.3 %shard_map.95 = bf16[1024,1024]{1,0:T(8,128)(2,1)} custom-call(bf16[2048,2048]{1,0:T(8,128)(2,1)} %bitcast.60, bf16[1024,1024]{1,0:T(8,128)(2,1)} %collective-permute-done.other_ref, bf16[2048,2048]{1,0:T(8,128)(2,1)} %bitcast.61), custom_call_target="tpu_custom_call" | custom-call | flops 60000002048 | bytes 8000000 | tf_op jit(solution)/shard_map/pallas_call | solution.py:181
  78.4 0.1 collective-permute-start.3
  78.5 2.3 fusion.46
  80.8 0.2 copy-done.4
  81.1 1.1 fusion.48
  82.2 0.6 collective-permute-done.3
  82.8 1.2 fusion.47
  84.0 3.2 %subtract_convert_fusion.2 = bf16[512,1024]{1,0:T(8,128)(2,1)S(1)} fusion(f32[512,512]{1,0:T(8,128)S(1)} %get-tuple-element.10, bf16[512,1024]{1,0:T(8,128)(2,1)S(1)} %get-tuple-element.14, pred[]{:T(512)S(6)} %eq.5, bf16[512,1024]{1,0:T(8,128)(2,1)S(1)} %get-tuple-element.12), kind=kOutput, calls=%fused_computation.42 | convolution fusion | flops 1084751872 | bytes 4194305 | tf_op jit(solution)/shard_map/dot_general | solution.py:200
  87.2 0.1 collective-permute-start.4
  87.3 25.2 %collective-permute-done.4 = bf16[512,1024]{1,0:T(8,128)(2,1)S(1)} collective-permute-done((bf16[512,1024]{1,0:T(8,128)(2,1)S(1)}, bf16[512,1024]{1,0:T(8,128)(2,1)S(1)}, u32[]{:S(2)}, u32[]{:S(2)}) %collective-permute-start.4) | collective-permute-done | bytes 1048608 | tf_op jit(solution)/shard_map/ppermute | solution.py:23
  112.5 0.4 convert_add_fusion
  112.9 0.1 collective-permute-start.5
  113.0 4.1 %subtract_convert_fusion.1.right_ref = bf16[1024,512]{1,0:T(8,128)(2,1)} fusion(f32[512,512]{1,0:T(8,128)S(1)} %get-tuple-element.9, pred[]{:T(512)S(6)} %eq.5, bf16[512,1024]{1,0:T(8,128)(2,1)S(1)} %get-tuple-element.12, bf16[512,1024]{1,0:T(8,128)(2,1)S(1)} %get-tuple-element.14, bf16[1024,1024]{1,0:T(8,128)(2,1)S(1)} %copy-done.4), kind=kOutput, calls=%fused_computation.40 | convolution fusion | flops 1084751872 | bytes 5243904 | tf_op jit(solution)/shard_map/dot_general | solution.py:200
  117.1 0.0 collective-permute-done.5
  117.1 2.4 maximum_select_fusion.own_ref
  119.5 1.6 broadcast_in_dim.24.other_ref
  121.1 35.4 %shard_map.96 = bf16[512,1024]{1,0:T(8,128)(2,1)} custom-call(f32[1024,1024]{1,0:T(8,128)} %maximum_select_fusion.own_ref, bf16[1024,1024]{1,0:T(8,128)(2,1)} %broadcast_in_dim.24.other_ref, bf16[1024,512]{1,0:T(8,128)(2,1)} %subtract_convert_fusion.1.right_ref), custom_call_target="tpu_custom_call" | custom-call | flops 60000002048 | bytes 8000000 | tf_op jit(solution)/shard_map/pallas_call | solution.py:181
  156.5 0.5 collective-permute-start.6
  157.0 2.5 collective-permute-done.6
  159.5 2.7 %maximum_select_fusion.10 = bf16[1024,1024]{1,0:T(8,128)(2,1)S(1)} fusion(bf16[512,1024]{1,0:T(8,128)(2,1)S(1)} %collective-permute-done.6, bf16[512,1024]{1,0:T(8,128)(2,1)} %shard_map.96, pred[]{:T(512)S(6)} %eq.5), kind=kLoop, calls=%fused_computation.39 | loop fusion | flops 9437184 | bytes 4194305 | tf_op jit(solution)/shard_map/jit(_where)/select_n | solution.py:40
  162.2 0.4 collective-permute-start.7
  162.6 0.0 reduce-scatter.2.cloned.1.call-update
  162.6 4.0 %fusion.25 = f32[512,1024]{1,0:T(8,128)S(1)} fusion(bf16[512,1024]{1,0:T(8,128)(2,1)} %get-tuple-element.13, bf16[512,1024]{1,0:T(8,128)(2,1)} %get-tuple-element.11, pred[]{:T(512)S(6)} %eq.5, f32[512,512]{1,0:T(8,128)S(1)} %get-tuple-element.8), kind=kOutput, calls=%fused_computation.51 | convolution fusion | flops 1085276160 | bytes 5242881 | tf_op jit(solution)/shard_map/dot_general | solution.py:200
  166.6 53.6 %collective-permute-done.7 = bf16[1024,1024]{1,0:T(8,128)(2,1)} collective-permute-done((bf16[1024,1024]{1,0:T(8,128)(2,1)S(1)}, bf16[1024,1024]{1,0:T(8,128)(2,1)}, u32[]{:S(2)}, u32[]{:S(2)}) %collective-permute-start.7) | collective-permute-done | bytes 2097184 | tf_op jit(solution)/shard_map/ppermute | solution.py:23
  220.2 6.0 %fusion.7 = bf16[1,512,2048]{2,1,0:T(8,128)(2,1)} fusion(bf16[512,1024]{1,0:T(8,128)(2,1)S(1)} %copy-done.5, bf16[1024,1024]{1,0:T(8,128)(2,1)} %collective-permute-done.7, bf16[1024,1024]{1,0:T(8,128)(2,1)S(1)} %maximum_select_fusion.10, pred[]{:T(512)S(6)} %eq.4, f32[512,1024]{1,0:T(8,128)S(1)} %fusion.25), kind=kOutput, calls=%fused_computation.18 | convolution fusion | flops 2169503744 | bytes 9437185 | tf_op jit(solution)/shard_map/dot_general | solution.py:200
  226.2 28.7 %reduce-scatter.2.cloned.1.call-done = f32[64,512]{1,0:T(8,128)} async-done(((f32[512,512]{1,0:T(8,128)}), f32[64,512]{1,0:T(8,128)}) %reduce-scatter.2.cloned.1.call-update) | async-done | bytes 131088 | tf_op jit(solution)/shard_map/reduce_scatter | solution.py:307
  (20 shorter events, 0.1 us)
Async XLA Ops:
  7.2 247.7 %reduce-scatter.2.cloned.1.call-start = ((), (), s32[]{:S(2)}) async-start(), calls=%async_computation.1 | async-start | bytes 1179648 | tf_op jit(solution)/shard_map/reduce_scatter | solution.py:307
  8.0 27.5 %collective-permute-start.1 = (bf16[2,1,1,512]{3,2,1,0:T(2,128)(2,1)S(1)}, bf16[2,1,1,512]{3,2,1,0:T(2,128)(2,1)S(1)}, u32[]{:S(2)}, u32[]{:S(2)}) collective-permute-start(bf16[2,1,1,512]{3,2,1,0:T(2,128)(2,1)S(1)} %get-tuple-element.15), channel_id=1, source_target_pairs={{0,8},{8,16},{16,24},{24,32},{32,40},{40,48},{48,56},{56,64},{64,7... | collective-permute-start | bytes 6152 | tf_op jit(solution)/shard_map/ppermute | solution.py:31
  9.9 25.6 %collective-permute-start.2 = (bf16[2,1,1,512]{3,2,1,0:T(2,128)(2,1)S(1)}, bf16[2,1,1,512]{3,2,1,0:T(2,128)(2,1)S(1)}, u32[]{:S(2)}, u32[]{:S(2)}) collective-permute-start(bf16[2,1,1,512]{3,2,1,0:T(2,128)(2,1)S(1)} %get-tuple-element.16), channel_id=1, source_target_pairs={{8,0},{16,8},{24,16},{32,24},{40,32},{48,40},{56,48},{64,56},{72,6... | collective-permute-start | bytes 6152 | tf_op jit(solution)/shard_map/ppermute | solution.py:34
  16.2 5.7 %copy-start = (bf16[1,512,512]{2,1,0:T(8,128)(2,1)S(1)}, bf16[1,512,512]{2,1,0:T(8,128)(2,1)}, u32[]{:S(2)}) copy-start(bf16[1,512,512]{2,1,0:T(8,128)(2,1)} %param.13) | copy-start | bytes 1572868
  16.3 5.7 %copy-start.1 = (bf16[1,512,512]{2,1,0:T(8,128)(2,1)S(1)}, bf16[1,512,512]{2,1,0:T(8,128)(2,1)}, u32[]{:S(2)}) copy-start(bf16[1,512,512]{2,1,0:T(8,128)(2,1)} %param.12) | copy-start | bytes 1572868
  21.9 0.7 copy-start.7
  22.0 20.2 %collective-permute-start = (bf16[1024,1024]{1,0:T(8,128)(2,1)}, bf16[1024,1024]{1,0:T(8,128)(2,1)}, u32[]{:S(2)}, u32[]{:S(2)}) collective-permute-start(bf16[1024,1024]{1,0:T(8,128)(2,1)} %get-tuple-element.6), channel_id=1, source_target_pairs={{0,8},{8,0},{16,24},{24,16},{32,40},{40,32},{48,56},{56,48},{64,72... | collective-permute-start | bytes 6291464 | tf_op jit(solution)/shard_map/ppermute | solution.py:23
  22.6 5.2 %copy-start.8 = (bf16[1,256]{1,0:T(2,128)(2,1)S(1)}, bf16[1,256]{1,0:T(2,128)(2,1)}, u32[]{:S(2)}) copy-start(bf16[1,256]{1,0:T(2,128)(2,1)} %param.15) | copy-start | bytes 1540
  35.5 1.2 copy-start.2
  36.7 3.7 %copy-start.3 = (f32[1,512,512]{2,1,0:T(8,128)S(1)}, f32[1,512,512]{2,1,0:T(8,128)}, u32[]{:S(2)}) copy-start(f32[1,512,512]{2,1,0:T(8,128)} %reshape.170) | copy-start | bytes 3145732
  36.7 3.7 %copy-start.6 = (bf16[1,512,512]{2,1,0:T(8,128)(2,1)S(1)}, bf16[1,512,512]{2,1,0:T(8,128)(2,1)}, u32[]{:S(2)}) copy-start(bf16[1,512,512]{2,1,0:T(8,128)(2,1)} %param.11) | copy-start | bytes 1572868
  78.4 4.4 %collective-permute-start.3 = (bf16[1024,1024]{1,0:T(8,128)(2,1)}, bf16[1024,1024]{1,0:T(8,128)(2,1)S(1)}, u32[]{:S(2)}, u32[]{:S(2)}) collective-permute-start(bf16[1024,1024]{1,0:T(8,128)(2,1)} %shard_map.95), channel_id=1, source_target_pairs={{0,8},{8,0},{16,24},{24,16},{32,40},{40,32},{48,56},{56,48},{64,72... | collective-permute-start | bytes 6291464 | tf_op jit(solution)/shard_map/ppermute | solution.py:23
  78.5 2.5 copy-start.4
  87.2 25.3 %collective-permute-start.4 = (bf16[512,1024]{1,0:T(8,128)(2,1)S(1)}, bf16[512,1024]{1,0:T(8,128)(2,1)S(1)}, u32[]{:S(2)}, u32[]{:S(2)}) collective-permute-start(bf16[512,1024]{1,0:T(8,128)(2,1)S(1)} %subtract_convert_fusion.2), channel_id=1, source_target_pairs={{0,16},{16,0},{8,24},{24,8},{32,48},{48,32},{40,56},{56,40},{64,80... | collective-permute-start | bytes 3145736 | tf_op jit(solution)/shard_map/ppermute | solution.py:23
  112.9 4.3 %collective-permute-start.5 = (f32[512,1024]{1,0:T(8,128)S(1)}, f32[512,1024]{1,0:T(8,128)S(1)}, u32[]{:S(2)}, u32[]{:S(2)}) collective-permute-start(f32[512,1024]{1,0:T(8,128)S(1)} %convert_add_fusion), channel_id=1, source_target_pairs={{0,8},{8,0},{16,24},{24,16},{32,40},{40,32},{48,56},{56,48},{64,72... | collective-permute-start | bytes 6291464 | tf_op jit(solution)/shard_map/ppermute | solution.py:23
  156.5 3.0 %collective-permute-start.6 = (bf16[512,1024]{1,0:T(8,128)(2,1)}, bf16[512,1024]{1,0:T(8,128)(2,1)S(1)}, u32[]{:S(2)}, u32[]{:S(2)}) collective-permute-start(bf16[512,1024]{1,0:T(8,128)(2,1)} %shard_map.96), channel_id=1, source_target_pairs={{0,8},{8,0},{16,24},{24,16},{32,40},{40,32},{48,56},{56,48},{64,72... | collective-permute-start | bytes 3145736 | tf_op jit(solution)/shard_map/ppermute | solution.py:23
  162.2 58.0 %collective-permute-start.7 = (bf16[1024,1024]{1,0:T(8,128)(2,1)S(1)}, bf16[1024,1024]{1,0:T(8,128)(2,1)}, u32[]{:S(2)}, u32[]{:S(2)}) collective-permute-start(bf16[1024,1024]{1,0:T(8,128)(2,1)S(1)} %maximum_select_fusion.10), channel_id=1, source_target_pairs={{0,16},{16,0},{8,24},{24,8},{32,48},{48,32},{40,56},{56,40},{64,80... | collective-permute-start | bytes 6291464 | tf_op jit(solution)/shard_map/ppermute | solution.py:23
  162.6 57.6 %copy-start.5 = (bf16[512,1024]{1,0:T(8,128)(2,1)S(1)}, bf16[512,1024]{1,0:T(8,128)(2,1)}, u32[]{:S(2)}) copy-start(bf16[512,1024]{1,0:T(8,128)(2,1)} %shard_map.96) | copy-start | bytes 3145732
Sparse Core Ops, SparseCore 0:
  162.7 92.1 reduce-scatter.1
